TPU v7x, 256 devices: a whole 4x4x8 slice. The times are simulated.
256 devices in a mesh: blk: 32 (over y_hi, z, core), phase: 8 (over y_lo, x).
Axes of the slice: x: 4, y: 4 (y_hi: 2, y_lo: 2; y = y_hi * 2 + y_lo), z: 8, core: 2. Of those that a mesh axis runs over, the one named last changes fastest.
Arguments:
- acts: bfloat16 [8, 4096, 2048], P('phase', 'blk'), may hold values from -6 to 6
- order: int32 [4096], replicated, may hold values from 0 to 4095, each once
- doc_ids: int32 [4096], replicated, may hold values from 0 to 7, never falling along the last dimension, each value on 1 to 1024 neighbouring positions
- gain: float32 [8, 2048], P('phase'), may hold values from 0.1 to 1.9
- w_query: bfloat16 [8, 2048, 1024], P('phase'), may hold values from -0.125 to 0.125
- w_keyval: bfloat16 [8, 2048, 2048], P('phase', 'blk'), may hold values from -0.125 to 0.125
- w_out: bfloat16 [8, 1024, 2048], P('phase'), may hold values from -0.5 to 0.5
- head_temp: float32 [8, 8], P('phase'), may hold values from 1 to 400
Outputs:
- layer_out: bfloat16 [8, 4096, 2048], P('phase', 'blk')
- next_input: bfloat16 [8, 4096, 2048], P('phase', 'blk')
Inputs may be any that keep to these rules, and one draw needn't show every extreme that they name: order holds every position of the sequence once. doc_ids never falls along positions; each document covers 1 to 1024 positions and one covers exactly 1024.
All inputs are finite; a program needn't handle non-finite values.
Results may differ from a plain program's by a relative error of at most 0.006.
The roundings to bfloat16 on the way count: a program that leaves them out, or rounds other values in their place, can miss the bound.
Values may be sent and summed in bfloat16 or wider, within the bound.
No kernel may reach another device: no remote copies, remote signals or barrier semaphores. Data moves between devices by JAX's collectives and lax.ppermute only.
A program may use at most 128 MiB of HBM per device.

v0:
```python
import jax
import jax.numpy as jnp
from jax import lax
from jax.sharding import PartitionSpec as P

mask_floor = -1e30


def passed_along(block, axis, distance):
    devices = range(lax.axis_size(axis))
    route = [(i - distance, i) for i in devices if i - distance in devices]
    return lax.ppermute(block, axis, route)


def per_device(acts, order, doc_ids, gain, w_query, w_keyval, w_out, head_temp):
    inputs = acts[0]
    tok_rows = inputs.shape[0]
    attn_width = w_query.shape[2]
    head_count = head_temp.shape[1]
    head_dim = attn_width // head_count
    block_index = lax.axis_index("blk")
    own_positions = lax.dynamic_slice_in_dim(order, block_index * tok_rows, tok_rows)
    own_docs = jnp.take(doc_ids, own_positions)
    upcast = inputs.astype(jnp.float32)
    normed = (
        upcast
        * lax.rsqrt(jnp.mean(upcast * upcast, axis=-1, keepdims=True) + 1e-05)
        * gain[0][None, :]
    ).astype(jnp.bfloat16)
    queries = jnp.dot(normed, w_query[0], preferred_element_type=jnp.float32)
    keyval = jnp.dot(
        normed,
        lax.all_gather(w_keyval[0], "blk", axis=0, tiled=True),
        preferred_element_type=jnp.float32,
    )
    query_heads = queries.reshape(tok_rows, head_count, head_dim)
    q_norm = (
        query_heads
        * lax.rsqrt(jnp.mean(query_heads * query_heads, axis=-1, keepdims=True) + 1e-06)
        * head_temp[0][None, :, None]
        / head_dim
    ).astype(jnp.bfloat16)
    key_heads = keyval[:, :attn_width].reshape(tok_rows, head_count, head_dim)
    k_norm = (
        (key_heads * lax.rsqrt(jnp.mean(key_heads * key_heads, axis=-1, keepdims=True) + 1e-06))
        .astype(jnp.bfloat16)
        .reshape(tok_rows, attn_width)
    )
    packed = jnp.concatenate([k_norm, keyval[:, attn_width:].astype(jnp.bfloat16)], axis=1)
    piece = lax.all_gather(packed, "blk", axis=0, tiled=True)
    peak = jnp.full((head_count, tok_rows), mask_floor, jnp.float32)
    count = piece.shape[0]
    key_doc = jnp.take(doc_ids, order)
    visible = (order[None, :] <= own_positions[:, None]) & (key_doc[None, :] == own_docs[:, None])
    remote_keys = piece[:, :attn_width].reshape(count, head_count, head_dim)
    remote_values = piece[:, attn_width:].reshape(count, head_count, head_dim).astype(jnp.float32)
    scores = jnp.einsum("qhd,khd->hqk", q_norm, remote_keys, preferred_element_type=jnp.float32)
    scores = jnp.where(visible[None], scores, mask_floor)
    new_peak = jnp.maximum(peak, jnp.max(scores, axis=-1))
    weights = jnp.where(visible[None], jnp.exp(scores - new_peak[..., None]), 0.0)
    total = jnp.sum(weights, axis=-1)
    accum = jnp.einsum(
        "hqk,khd->hqd",
        weights,
        remote_values,
        precision=lax.Precision.HIGHEST,
        preferred_element_type=jnp.float32,
    )
    peak, total, accum = (new_peak, total, accum)
    mixed = (
        (accum / total[..., None])
        .transpose(1, 0, 2)
        .reshape(tok_rows, attn_width)
        .astype(jnp.bfloat16)
    )
    produced = (upcast + jnp.dot(mixed, w_out[0], preferred_element_type=jnp.float32)).astype(
        jnp.bfloat16
    )
    handed = passed_along(produced, "phase", 1)
    return (produced[None], handed[None])


def solution(mesh):
    return jax.shard_map(
        per_device,
        mesh=mesh,
        in_specs=(
            P("phase", "blk", None),
            P(),
            P(),
            P("phase", None),
            P("phase", None, None),
            P("phase", "blk", None),
            P("phase", None, None),
            P("phase", None),
        ),
        out_specs=(P("phase", "blk", None), P("phase", "blk", None)),
        check_vma=False,
    )
```

profile of v0, /device:TPU:8, one launch (start us, length us, event | category | flops | bytes accessed | tf_op | source)
XLA Modules:
  0.0 339.7 jit_solution(15806795730808162947)
XLA Ops:
  7.2 0.7 all-gather.6.cloned.1.call-update
  8.0 1.2 fusion.22
  9.2 105.0 %all-gather.6.cloned.1.call-done = bf16[1,2048,2048]{2,1,0:T(8,128)(2,1)} async-done(((bf16[1,64,2048]{2,1,0:T(8,128)(2,1)}), bf16[1,2048,2048]{2,1,0:T(8,128)(2,1)}) %all-gather.6.cloned.1.call-update) | async-done | bytes 8388624 | tf_op jit(solution)/shard_map/all_gather | solution.py:33
  114.2 4.9 %fusion.5 = f32[128,2048]{1,0:T(8,128)S(1)} fusion(bf16[1,2048,2048]{2,1,0:T(8,128)(2,1)} %all-gather.6.cloned.1.call-done, bf16[1,128,2048]{2,1,0:T(8,128)(2,1)} %param.8, f32[2048]{0:T(1024)} %bitcast.74, f32[128]{0:T(128)S(1)} %add_rsqrt_fusion.2), kind=kOutput, calls=%fused_computation.10 | convolution fusion | flops 1074790400 | bytes 9970176 | tf_op jit(solution)/shard_map/dot_general | solution.py:31
  119.3 0.2 reduce_sum.38
  119.7 0.2 mul.91
  119.9 0.1 fusion.33
  120.1 0.8 pad_maximum_fusion
  121.0 1.1 gather_fusion.1
  122.2 23.0 %gather_fusion = s32[4096]{0:T(1024)S(1)} fusion(s32[4096]{0:T(1024)S(1)} %copy-done, s32[4096]{0:T(1024)S(1)} %fusion.41), kind=kCustom, calls=%fused_computation | custom fusion | bytes 49152 | tf_op jit(solution)/shard_map/jit(_take)/gather | solution.py:53
  145.3 6.6 %copy.32 = bf16[1024,2048]{1,0:T(8,128)(2,1)} copy(bf16[1024,2048]{0,1:T(8,128)(2,1)} %bitcast.68) | data formatting | bytes 8388608 | tf_op jit(solution)/shard_map/dot_general | solution.py:30
  151.9 4.4 %multiply_reduce_fusion = (f32[128,8]{0,1:T(8,128)S(1)}, f32[128,8,128]{0,2,1:T(8,128)}) fusion(bf16[8,128,2048]{2,1,0:T(8,128)(2,1)} %bitcast.66, bf16[1,128,2048]{2,1,0:T(8,128)(2,1)S(1)} %copy-done.3, f32[2048]{0:T(1024)S(1)} %bitcast.75, f32[128]{0:T(128)S(1)} %add_rsqrt_fusion.2), kind=kOutput, calls=%fused_computation.43 | convolution fusion | flops 538180608 | bytes 5255680 | tf_op jit(solution)/shard_map/dot_general | solution.py:30
  156.3 1.3 compare_and_fusion
  157.6 97.7 %all-gather.4.cloned.1.call-done = bf16[4096,2048]{1,0:T(8,128)(2,1)} async-done(((bf16[128,2048]{1,0:T(8,128)(2,1)}), bf16[4096,2048]{1,0:T(8,128)(2,1)}) %all-gather.4.cloned.1.call-update) | async-done | bytes 16777232 | tf_op jit(solution)/shard_map/all_gather | solution.py:50
  255.3 10.1 %slice_bitcast_fusion = (bf16[512,8,8,128]{3,2,1,0:T(8,128)(2,1)S(1)}, bf16[4096,1024]{1,0:T(8,128)(2,1)}) fusion(bf16[4096,2048]{1,0:T(8,128)(2,1)} %all-gather.4.cloned.1.call-done), kind=kLoop, calls=%fused_computation.9 | loop fusion | bytes 33554432
  265.5 8.9 %select_reduce_fusion = (f32[8,128]{1,0:T(8,128)S(1)}, f32[8,128,4096]{2,1,0:T(8,128)}) fusion(pred[128,4096]{1,0:T(8,128)(4,1)} %compare_and_fusion, bf16[512,8,8,128]{3,2,1,0:T(8,128)(2,1)S(1)} %get-tuple-element.4, f32[128,8,128]{0,2,1:T(8,128)} %get-tuple-element.7, f32[8]{0:T(128)S(1)} %bitcast.77, f32[128,8]{0,1:T(8,128)S(1)} %add_rsqrt_fusion.1), kind=kOutput, calls=%fused_computation.3 | convolution fusion | flops 1082653696 | bytes 26222624 | tf_op jit(solution)/shard_map/qhd,khd->hqk/dot_general | solution.py:57
  274.4 11.2 %copy.33 = bf16[4096,1024]{0,1:T(8,128)(2,1)} copy(bf16[4096,1024]{1,0:T(8,128)(2,1)} %get-tuple-element.5) | data formatting | bytes 16777216 | tf_op jit(solution)/shard_map/reshape | solution.py:56
  285.6 8.7 %fusion = f32[8,128]{1,0:T(8,128)S(1)} fusion(f32[8,128,4096]{2,1,0:T(8,128)} %get-tuple-element.9, f32[8,128]{1,0:T(8,128)S(1)} %broadcast_maximum_fusion, pred[128,4096]{1,0:T(8,128)(4,1)} %compare_and_fusion), kind=kLoop, calls=%fused_computation.4 | loop fusion | flops 16776192 | bytes 17309696 | tf_op jit(solution)/shard_map/reduce_sum | solution.py:61
  294.3 2.2 copy-done.2
  296.5 14.5 %fusion.28 = bf16[128,8,128]{0,2,1:T(8,128)(2,1)S(1)} fusion(bf16[4096,8,128]{0,2,1:T(8,128)(2,1)} %bitcast.67, f32[8,128,4096]{2,1,0:T(8,128)S(1)} %copy-done.2, f32[8,128]{1,0:T(8,128)S(1)} %broadcast_maximum_fusion, pred[128,4096]{1,0:T(8,128)(4,1)} %compare_and_fusion, f32[128,8]{0,1:T(8,128)S(1)} %bitcast.76), kind=kOutput, calls=%fused_computation.32 | convolution fusion | flops 6455296000 | bytes 25960448 | tf_op jit(solution)/shard_map/hqk,khd->hqd/dot_general | solution.py:62
  311.0 2.9 fusion.16
  314.0 3.4 collective-permute-start
  317.3 14.7 %collective-permute-done = bf16[128,2048]{1,0:T(8,128)(2,1)S(1)} collective-permute-done((bf16[128,2048]{1,0:T(8,128)(2,1)S(1)}, bf16[128,2048]{1,0:T(8,128)(2,1)S(1)}, u32[]{:S(2)}, u32[]{:S(2)}) %collective-permute-start) | collective-permute-done | bytes 524320 | tf_op jit(solution)/shard_map/ppermute | solution.py:12
  332.0 0.8 copy.45
  (32 shorter events, 0.6 us)
Async XLA Ops:
  7.2 113.9 %copy-start = (s32[4096]{0:T(1024)S(1)}, s32[4096]{0:T(1024)}, u32[]{:S(2)}) copy-start(s32[4096]{0:T(1024)} %param.10) | copy-start | bytes 49156
  7.2 107.1 %all-gather.6.cloned.1.call-start = ((), (), s32[]{:S(2)}) async-start(), calls=%async_computation.1 | async-start | bytes 8650752 | tf_op jit(solution)/shard_map/all_gather | solution.py:33
  7.9 247.4 %all-gather.4.cloned.1.call-start = ((), (), s32[]{:S(2)}) async-start(), calls=%async_computation | async-start | bytes 17301504 | tf_op jit(solution)/shard_map/all_gather | solution.py:50
  114.2 6.7 %copy-start.5 = (s32[4096]{0:T(1024)S(1)}, s32[4096]{0:T(1024)}, u32[]{:S(2)}) copy-start(s32[4096]{0:T(1024)} %param.9) | copy-start | bytes 49156
  145.2 6.7 %copy-start.3 = (bf16[1,128,2048]{2,1,0:T(8,128)(2,1)S(1)}, bf16[1,128,2048]{2,1,0:T(8,128)(2,1)}, u32[]{:S(2)}) copy-start(bf16[1,128,2048]{2,1,0:T(8,128)(2,1)} %param.8) | copy-start | bytes 1572868
  145.3 6.7 %copy-start.6 = (f32[1,2048]{1,0:T(1,128)S(1)}, f32[1,2048]{1,0:T(1,128)}, u32[]{:S(2)}) copy-start(f32[1,2048]{1,0:T(1,128)} %param.11) | copy-start | bytes 24580
  157.6 107.9 %copy-start.7 = (f32[1,8]{1,0:T(1,128)S(1)}, f32[1,8]{1,0:T(1,128)}, u32[]{:S(2)}) copy-start(f32[1,8]{1,0:T(1,128)} %param.15) | copy-start | bytes 100
  285.6 10.9 %copy-start.2 = (f32[8,128,4096]{2,1,0:T(8,128)S(1)}, f32[8,128,4096]{2,1,0:T(8,128)}, u32[]{:S(2)}) copy-start(f32[8,128,4096]{2,1,0:T(8,128)} %get-tuple-element.9) | copy-start | bytes 50331652
  296.5 36.3 %copy-start.1 = (s32[4096]{0:T(1024)S(1)}, s32[4096]{0:T(1024)}, u32[]{:S(2)}) copy-start(s32[4096]{0:T(1024)} %param.10) | copy-start | bytes 49156
  313.9 18.9 %copy-start.4 = (bf16[128,2048]{1,0:T(8,128)(2,1)}, bf16[128,2048]{1,0:T(8,128)(2,1)S(1)}, u32[]{:S(2)}) copy-start(bf16[128,2048]{1,0:T(8,128)(2,1)S(1)} %fusion.16) | copy-start | bytes 1572868
  314.0 18.1 %collective-permute-start = (bf16[128,2048]{1,0:T(8,128)(2,1)S(1)}, bf16[128,2048]{1,0:T(8,128)(2,1)S(1)}, u32[]{:S(2)}, u32[]{:S(2)}) collective-permute-start(bf16[128,2048]{1,0:T(8,128)(2,1)S(1)} %fusion.16), channel_id=1, source_target_pairs={{0,1},{1,2},{2,3},{3,4},{4,5},{5,6},{6,7},{8,9},{9,10},{10,11},{11... | collective-permute-start | bytes 1572872 | tf_op jit(solution)/shard_map/ppermute | solution.py:12
Sparse Core Ops, SparseCore 0:
  10.8 103.4 all-gather.5
  121.0 134.2 all-gather.3
where the time goes:
time: 340 us
  waiting for transfers between devices  218 us (64%)
  local copies, waits for them, and re-layouts  55.7 us (16%)
  matrix products  35.6 us (10%)
  between operations  14.2 us (4%)
  other arithmetic  12.5 us (4%)
  starting transfers between devices  3.45 us (1%)
    all_gather x1, waiting for transfers between devices, per_device(): lax.all_gather(w_keyval[0], 'blk', axis=0, tiled=True)  105 us
    all_gather x1, waiting for transfers between devices, per_device(): piece = lax.all_gather(packed, 'blk', axis=0, tiled=True)  97.7 us
    gather x1, local copies, waits for them, and re-layouts, per_device(): key_doc = jnp.take(doc_ids, order)  23 us
    ppermute x1, waiting for transfers between devices, passed_along(): return lax.ppermute(block, axis, route)  14.7 us
    dot_general x1, matrix products, per_device(): jnp.einsum('hqk,khd->hqd', weights, remote_values, precision=lax.Precisio...  14.5 us
    unnamed x19, local copies, waits for them, and re-layouts  13.3 us
    reshape x1, local copies, waits for them, and re-layouts, per_device(): piece[:, attn_width:].reshape(count, head_count, head_dim)  11.2 us
    dot_general x1, matrix products, per_device(): jnp.einsum('qhd,khd->hqk', q_norm, remote_keys, preferred_element_type=jn...  8.92 us
  transfers between devices with their start and end apart: 3, of which 3 were waited for; matrix products, arithmetic and copies ran while one was open for 11% of the time, Pallas kernels for 0%

commit v1 on v0

--- a/solution.py
+++ b/solution.py
@@ -30,7 +30,9 @@
     queries = jnp.dot(normed, w_query[0], preferred_element_type=jnp.float32)
     keyval = jnp.dot(
         normed,
-        lax.all_gather(w_keyval[0], "blk", axis=0, tiled=True),
+        jnp.concatenate(
+            lax.all_to_all(jnp.stack([w_keyval[0]] * lax.axis_size("blk")), "blk", 0, 0), axis=0
+        ),
         preferred_element_type=jnp.float32,
     )
     query_heads = queries.reshape(tok_rows, head_count, head_dim)

time: 340 us -> 441 us (1.30)
  waiting for transfers between devices: 218 us -> 303 us
  starting transfers between devices: 3.45 us -> 14.3 us
  local copies, waits for them, and re-layouts: 55.7 us -> 61.6 us
    all_to_all x0 -> x1, waiting for transfers between devices: none -> 187 us  [per_device(): lax.all_to_all(jnp.stack([w_keyval[0]] * lax.axis_size('blk')), 'blk', 0, 0)]
    all_gather x1 -> x0, waiting for transfers between devices: 105 us -> none  [per_device(): lax.all_gather(w_keyval[0], 'blk', axis=0, tiled=True)]
    all_to_all x0 -> x1, starting transfers between devices: none -> 10.8 us  [per_device(): lax.all_to_all(jnp.stack([w_keyval[0]] * lax.axis_size('blk')), 'blk', 0, 0)]
    another operation x0 -> x1, local copies, waits for them, and re-layouts: none -> 5.24 us  [per_device(): jnp.stack([w_keyval[0]] * lax.axis_size('blk'))]
  transfers between devices with their start and end apart: 3 -> 3, of which waited for: 3 -> 3; matrix products, arithmetic and copies ran while one was open for 11% -> 8% of each run, Pallas kernels for 0% -> 0%
where the time goes in v1:
time: 441 us; the launch traced here: 440 us
  waiting for transfers between devices  303 us (69%)
  local copies, waits for them, and re-layouts  61.6 us (14%)
  matrix products  35.3 us (8%)
  starting transfers between devices  14.3 us (3%)
  between operations  14.2 us (3%)
  other arithmetic  11.5 us (3%)
    all_to_all x1, waiting for transfers between devices, per_device(): lax.all_to_all(jnp.stack([w_keyval[0]] * lax.axis_size('blk')), 'blk', 0, 0)  187 us
    all_gather x1, waiting for transfers between devices, per_device(): piece = lax.all_gather(packed, 'blk', axis=0, tiled=True)  101 us
    gather x1, local copies, waits for them, and re-layouts, per_device(): key_doc = jnp.take(doc_ids, order)  23 us
    ppermute x1, waiting for transfers between devices, passed_along(): return lax.ppermute(block, axis, route)  14.7 us
    dot_general x1, matrix products, per_device(): jnp.einsum('hqk,khd->hqd', weights, remote_values, precision=lax.Precisio...  14.5 us
    unnamed x19, local copies, waits for them, and re-layouts  13.3 us
    reshape x1, local copies, waits for them, and re-layouts, per_device(): piece[:, attn_width:].reshape(count, head_count, head_dim)  12 us
    all_to_all x1, starting transfers between devices, per_device(): lax.all_to_all(jnp.stack([w_keyval[0]] * lax.axis_size('blk')), 'blk', 0, 0)  10.8 us
  transfers between devices with their start and end apart: 3, of which 3 were waited for; matrix products, arithmetic and copies ran while one was open for 8% of the time, Pallas kernels for 0%

profile of v1, /device:TPU:8, one launch (start us, length us, event | category | flops | bytes accessed | tf_op | source)
XLA Modules:
  0.0 439.9 jit_solution(10694609359792793322)
XLA Ops:
  7.2 5.2 %stack.3 = bf16[32,64,2048]{2,1,0:T(8,128)(2,1)} broadcast(bf16[64,2048]{1,0:T(8,128)(2,1)} %bitcast.68), dimensions={1,2} | broadcast | bytes 8650752 | tf_op jit(solution)/shard_map/stack | solution.py:34
  12.4 10.8 %all-to-all-start = ((bf16[32,64,2048]{2,1,0:T(8,128)(2,1)}), bf16[32,64,2048]{2,1,0:T(8,128)(2,1)}, u32[]{:S(2)}, u32[]{:S(2)}) async-start(bf16[32,64,2048]{2,1,0:T(8,128)(2,1)} %stack.3), calls=%async_computation | async-start | bytes 16777216 | tf_op jit(solution)/shard_map/all_to_all | solution.py:34
  23.3 0.2 fusion.19
  23.5 187.4 %all-to-all-done = bf16[32,64,2048]{2,1,0:T(8,128)(2,1)} async-done(((bf16[32,64,2048]{2,1,0:T(8,128)(2,1)}), bf16[32,64,2048]{2,1,0:T(8,128)(2,1)}, u32[]{:S(2)}, u32[]{:S(2)}) %all-to-all-start) | async-done | bytes 8388640 | tf_op jit(solution)/shard_map/all_to_all | solution.py:34
  210.9 4.7 %fusion.27 = f32[128,2048]{1,0:T(8,128)S(1)} fusion(bf16[2048,2048]{1,0:T(8,128)(2,1)} %bitcast.9, bf16[1,128,2048]{2,1,0:T(8,128)(2,1)S(1)} %copy-done.3, f32[2048]{0:T(1024)S(1)} %bitcast.70, f32[128]{0:T(128)S(1)} %add_rsqrt_fusion.2), kind=kOutput, calls=%fused_computation.34 | convolution fusion | flops 1074790400 | bytes 9970176 | tf_op jit(solution)/shard_map/dot_general | solution.py:31
  215.8 0.2 reduce_sum.38
  216.2 0.2 mul.81
  216.6 0.8 pad_maximum_fusion
  217.5 1.1 gather_fusion.1
  218.7 23.0 %gather_fusion = s32[4096]{0:T(1024)S(1)} fusion(s32[4096]{0:T(1024)S(1)} %copy-done, s32[4096]{0:T(1024)S(1)} %fusion.34), kind=kCustom, calls=%fused_computation | custom fusion | bytes 49152 | tf_op jit(solution)/shard_map/jit(_take)/gather | solution.py:55
  241.7 6.5 %copy.32 = bf16[1024,2048]{1,0:T(8,128)(2,1)} copy(bf16[1024,2048]{0,1:T(8,128)(2,1)} %bitcast.63) | data formatting | bytes 8388608 | tf_op jit(solution)/shard_map/dot_general | solution.py:30
  248.2 4.4 multiply_reduce_fusion
  252.6 1.3 compare_and_fusion
  253.9 101.0 %all-gather.2.cloned.1.call-done = bf16[4096,2048]{1,0:T(8,128)(2,1)} async-done(((bf16[128,2048]{1,0:T(8,128)(2,1)}), bf16[4096,2048]{1,0:T(8,128)(2,1)}) %all-gather.2.cloned.1.call-update) | async-done | bytes 16777232 | tf_op jit(solution)/shard_map/all_gather | solution.py:52
  354.9 10.1 %slice_bitcast_fusion = (bf16[512,8,8,128]{3,2,1,0:T(8,128)(2,1)S(1)}, bf16[4096,1024]{1,0:T(8,128)(2,1)}) fusion(bf16[4096,2048]{1,0:T(8,128)(2,1)} %all-gather.2.cloned.1.call-done), kind=kLoop, calls=%fused_computation.9 | loop fusion | bytes 33554432
  365.0 8.8 %select_reduce_fusion = (f32[8,128]{1,0:T(8,128)S(1)}, f32[8,128,4096]{2,1,0:T(8,128)}) fusion(pred[128,4096]{1,0:T(8,128)(4,1)} %compare_and_fusion, bf16[512,8,8,128]{3,2,1,0:T(8,128)(2,1)S(1)} %get-tuple-element.4, f32[128,8,128]{0,2,1:T(8,128)} %get-tuple-element.7, f32[8]{0:T(128)S(1)} %bitcast.73, f32[128,8]{0,1:T(8,128)S(1)} %add_rsqrt_fusion.1), kind=kOutput, calls=%fused_computation.3 | convolution fusion | flops 1082653696 | bytes 26222624 | tf_op jit(solution)/shard_map/qhd,khd->hqk/dot_general | solution.py:59
  373.8 12.0 %copy.33 = bf16[4096,1024]{0,1:T(8,128)(2,1)} copy(bf16[4096,1024]{1,0:T(8,128)(2,1)} %get-tuple-element.5) | data formatting | bytes 16777216 | tf_op jit(solution)/shard_map/reshape | solution.py:58
  385.8 8.7 %fusion = f32[8,128]{1,0:T(8,128)S(1)} fusion(f32[8,128,4096]{2,1,0:T(8,128)} %get-tuple-element.9, f32[8,128]{1,0:T(8,128)S(1)} %broadcast_maximum_fusion, pred[128,4096]{1,0:T(8,128)(4,1)} %compare_and_fusion), kind=kLoop, calls=%fused_computation.4 | loop fusion | flops 16776192 | bytes 17309696 | tf_op jit(solution)/shard_map/reduce_sum | solution.py:63
  394.5 2.2 copy-done.2
  396.7 14.5 %fusion.23 = bf16[128,8,128]{0,2,1:T(8,128)(2,1)S(1)} fusion(bf16[4096,8,128]{0,2,1:T(8,128)(2,1)} %bitcast.62, f32[8,128,4096]{2,1,0:T(8,128)S(1)} %copy-done.2, f32[8,128]{1,0:T(8,128)S(1)} %broadcast_maximum_fusion, pred[128,4096]{1,0:T(8,128)(4,1)} %compare_and_fusion, f32[128,8]{0,1:T(8,128)S(1)} %bitcast.72), kind=kOutput, calls=%fused_computation.27 | convolution fusion | flops 6455296000 | bytes 25960448 | tf_op jit(solution)/shard_map/hqk,khd->hqd/dot_general | solution.py:64
  411.2 2.9 fusion.14
  414.2 3.4 collective-permute-start
  417.5 14.7 %collective-permute-done = bf16[128,2048]{1,0:T(8,128)(2,1)S(1)} collective-permute-done((bf16[128,2048]{1,0:T(8,128)(2,1)S(1)}, bf16[128,2048]{1,0:T(8,128)(2,1)S(1)}, u32[]{:S(2)}, u32[]{:S(2)}) %collective-permute-start) | collective-permute-done | bytes 524320 | tf_op jit(solution)/shard_map/ppermute | solution.py:12
  432.3 0.8 copy.45
  (32 shorter events, 0.7 us)
Async XLA Ops:
  7.2 210.4 %copy-start = (s32[4096]{0:T(1024)S(1)}, s32[4096]{0:T(1024)}, u32[]{:S(2)}) copy-start(s32[4096]{0:T(1024)} %param.10) | copy-start | bytes 49156
  12.4 10.9 %copy-start.3 = (bf16[1,128,2048]{2,1,0:T(8,128)(2,1)S(1)}, bf16[1,128,2048]{2,1,0:T(8,128)(2,1)}, u32[]{:S(2)}) copy-start(bf16[1,128,2048]{2,1,0:T(8,128)(2,1)} %param.8) | copy-start | bytes 1572868
  12.4 198.5 %copy-start.6 = (f32[1,2048]{1,0:T(1,128)S(1)}, f32[1,2048]{1,0:T(1,128)}, u32[]{:S(2)}) copy-start(f32[1,2048]{1,0:T(1,128)} %param.11) | copy-start | bytes 24580
  12.4 198.5 %all-to-all-start = ((bf16[32,64,2048]{2,1,0:T(8,128)(2,1)}), bf16[32,64,2048]{2,1,0:T(8,128)(2,1)}, u32[]{:S(2)}, u32[]{:S(2)}) async-start(bf16[32,64,2048]{2,1,0:T(8,128)(2,1)} %stack.3), calls=%async_computation | async-start | bytes 16777216 | tf_op jit(solution)/shard_map/all_to_all | solution.py:34
  23.3 331.6 %all-gather.2.cloned.1.call-start = ((), (), s32[]{:S(2)}) async-start(), calls=%async_computation.1 | async-start | bytes 17301504 | tf_op jit(solution)/shard_map/all_gather | solution.py:52
  210.9 6.5 %copy-start.5 = (s32[4096]{0:T(1024)S(1)}, s32[4096]{0:T(1024)}, u32[]{:S(2)}) copy-start(s32[4096]{0:T(1024)} %param.9) | copy-start | bytes 49156
  253.9 111.1 %copy-start.7 = (f32[1,8]{1,0:T(1,128)S(1)}, f32[1,8]{1,0:T(1,128)}, u32[]{:S(2)}) copy-start(f32[1,8]{1,0:T(1,128)} %param.15) | copy-start | bytes 100
  385.8 10.9 %copy-start.2 = (f32[8,128,4096]{2,1,0:T(8,128)S(1)}, f32[8,128,4096]{2,1,0:T(8,128)}, u32[]{:S(2)}) copy-start(f32[8,128,4096]{2,1,0:T(8,128)} %get-tuple-element.9) | copy-start | bytes 50331652
  396.7 36.3 %copy-start.1 = (s32[4096]{0:T(1024)S(1)}, s32[4096]{0:T(1024)}, u32[]{:S(2)}) copy-start(s32[4096]{0:T(1024)} %param.10) | copy-start | bytes 49156
  414.1 18.9 %copy-start.4 = (bf16[128,2048]{1,0:T(8,128)(2,1)}, bf16[128,2048]{1,0:T(8,128)(2,1)S(1)}, u32[]{:S(2)}) copy-start(bf16[128,2048]{1,0:T(8,128)(2,1)S(1)} %fusion.14) | copy-start | bytes 1572868
  414.2 18.1 %collective-permute-start = (bf16[128,2048]{1,0:T(8,128)(2,1)S(1)}, bf16[128,2048]{1,0:T(8,128)(2,1)S(1)}, u32[]{:S(2)}, u32[]{:S(2)}) collective-permute-start(bf16[128,2048]{1,0:T(8,128)(2,1)S(1)} %fusion.14), channel_id=1, source_target_pairs={{0,1},{1,2},{2,3},{3,4},{4,5},{5,6},{6,7},{8,9},{9,10},{10,11},{11... | collective-permute-start | bytes 1572872 | tf_op jit(solution)/shard_map/ppermute | solution.py:12
Sparse Core Ops, SparseCore 0:
  217.5 137.2 all-gather.1
